TPU v7x, 256 devices: a whole 4x4x8 slice. The times are simulated.
256 devices in a mesh: gz: 4 (over y), row: 8 (over z), col: 8 (over x, core).
Axes of the slice: x: 4, y: 4, z: 8, core: 2. Of those that a mesh axis runs over, the one named last changes fastest.
Arguments:
- diag_parts: float32 [4, 512, 512], P('gz', 'row', 'col'), as said below
- column_parts: float32 [4, 8192, 512], P('gz', 'row', 'col'), may hold values from -6 to 6
- row_parts: float32 [4, 512, 8192], P('gz', 'row', 'col'), may hold values from -2.1 to 2.1
- schur_parts: float32 [4, 8192, 8192], P('gz', 'row', 'col'), may hold values from -6 to 6
- block_pattern: int32 [4, 64, 64], P('gz', 'row', 'col'), may hold values 0 or 1
- pivot_order: int32 [512], replicated, may hold values from 0 to 511, as said below
Outputs:
- factor_diag: float32 [512, 512], P('row', 'col')
- lower_panel: float32 [8192, 512], P('row', 'col')
- upper_panel: float32 [512, 8192], P('row', 'col')
- schur_out: float32 [8192, 8192], P('row', 'col')
Inputs may be any that keep to these rules, and one draw needn't show every extreme that they name: `pivot_order`: a permutation of 0 to 511. For every layer g the rows of diag_parts[g] taken in the order pivot_order form a symmetric matrix; the sum over layers so reordered is symmetric positive definite with smallest eigenvalue at least 8.
All inputs are finite; a program needn't handle non-finite values. No bound on the sum of `block_pattern` on one device may be relied on, other than what follows from the above.
Results may differ from a plain program's by a relative error of at most 0.00013.
Values sent between devices are 32-bit elements; how exact they have to be, the bound alone decides.
A program may use at most 64 MiB of HBM per device.

v0:
```python
import functools

import jax
import jax.numpy as jnp
from jax import lax
from jax.experimental import pallas as pl
from jax.experimental.pallas import tpu as pltpu
from jax.sharding import PartitionSpec as P

BS = 128
LAYERS = 4
PANEL = 16
HALF = PANEL + BS
SUBS = ((0, 16), (16, 32), (48, 32), (80, 32), (112, 32))
HI = lax.Precision.HIGHEST
F32 = jnp.float32
BF16 = jnp.bfloat16
MESH = pl.DeviceIdType.MESH


def split2(x):
    hi = x.astype(BF16)
    return hi, (x - hi.astype(F32)).astype(BF16)


def split3(x):
    hi = x.astype(BF16)
    rest = x - hi.astype(F32)
    mid = rest.astype(BF16)
    return hi, mid, (rest - mid.astype(F32)).astype(BF16)


def contract(a, b, da, db):
    return lax.dot_general(a, b, (((da,), (db,)), ((), ())), preferred_element_type=F32)


def dot3(a, b):
    return contract(a[0], b[0], 1, 0) + (contract(a[0], b[1], 1, 0) + contract(a[1], b[0], 1, 0))


def eliminate_group(d_ref, q):
    lane = lax.broadcasted_iota(jnp.int32, (8, 128), 1)
    sub = lax.broadcasted_iota(jnp.int32, (8, 128), 0)
    lo = 8 * q
    g = d_ref[lo : lo + 8, :]
    col = [jnp.broadcast_to(g[:, lo + j : lo + j + 1], (8, 128)) for j in range(8)]
    snap = jnp.zeros((8, 128), F32)
    pivots = jnp.ones((8, 128), F32)
    for k in range(8):
        piv = jnp.broadcast_to(col[k][k : k + 1, :], (8, 128))
        f = jnp.where(sub != k, col[k] * (1.0 / piv), 0.0)
        for j in range(k + 1, 8):
            col[j] = col[j] - f * jnp.broadcast_to(col[j][k : k + 1, :], (8, 128))
        g = jnp.where(lane == lo + k, jnp.where(sub == k, 1.0, 0.0), g)
        top = jnp.broadcast_to(g[k : k + 1, :], (8, 128))
        snap = jnp.where(sub == k, top, snap)
        pivots = jnp.where(sub == k, piv, pivots)
        g = g - f * top
    w = g / pivots
    if q < 15:
        below = d_ref[lo + 8 : lo + 16, :]
        acc = jnp.where((lane >= lo) & (lane < lo + 8), 0.0, below)
        for j in range(8):
            acc = acc - jnp.broadcast_to(below[:, lo + j : lo + j + 1], (8, 128)) * jnp.broadcast_to(
                w[j : j + 1, :], (8, 128)
            )
        d_ref[lo + 8 : lo + 16, :] = acc
    if q < 14:
        gh, gm, gl = (x.astype(F32) for x in split3(d_ref[lo : lo + 8, :]))
        wh, wm, wl = (x.astype(F32) for x in split3(w))
        update = contract(
            jnp.concatenate([gh, gh, gm, gh, gm, gl], axis=0).astype(BF16),
            jnp.concatenate([wh, wm, wh, wl, wm, wh], axis=0).astype(BF16),
            0,
            0,
        )
        rest = d_ref[lo + 16 : 128, :]
        lane_r = lax.broadcasted_iota(jnp.int32, rest.shape, 1)
        d_ref[lo + 16 : 128, :] = jnp.where((lane_r >= lo) & (lane_r < lo + 8), 0.0, rest) - update[lo + 16 :, :]
    d_ref[lo : lo + 8, :] = jnp.where(lane == lo + sub, 1.0, snap) * lax.rsqrt(pivots)
    return jnp.sqrt(pivots)


def eliminate_block(a_ref, d_ref, up_ref, i, hook):
    width = a_ref.shape[0]
    at = pl.multiple_of(i * 128, 128)
    rows = pl.ds(at, 128)
    d_ref[...] = a_ref[rows, pl.ds(at, 128)]
    diagonal = []
    for q in range(16):
        if q % 4 == 0:
            hook(i, q // 4)
        diagonal.append(eliminate_group(d_ref, q))
    r = lax.broadcasted_iota(jnp.int32, (128, 128), 0)
    c = lax.broadcasted_iota(jnp.int32, (128, 128), 1)
    d = d_ref[...]
    inverse = jnp.where(c <= r, d, 0.0)
    upper = jnp.where(c > r, d, jnp.where(c == r, jnp.concatenate(diagonal, axis=0), 0.0))
    up_ref[i] = upper
    a_ref[rows, :] = jnp.dot(inverse, a_ref[rows, :], precision=HI, preferred_element_type=F32)
    a_ref[rows, pl.ds(at, 128)] = inverse

    @pl.loop(i + 1, width // 128)
    def _(j):
        below = pl.ds(pl.multiple_of(j * 128, 128), 128)
        a_ref[below, pl.ds(at, 128)] = jnp.zeros((128, 128), F32)
        a_ref[below, :] = a_ref[below, :] - lax.dot_general(
            a_ref[rows, below], a_ref[rows, :], (((0,), (0,)), ((), ())), precision=HI, preferred_element_type=F32
        )


def kernel(
    grid_rows, grid_cols,
    diag_hbm, pattern_hbm, pivot_hbm, column_ref, row_ref, schur_ref,
    factor_out, lower_out, upper_out, update,
    diag_ref, pattern_ref, pivot_ref, w, fin, rs1, rsx, weights,
    layer_diag, grid_diag, full_diag, all_columns, all_rows, a_ref, d_ref, up_ref, left_x, right_x,
    load_sem, y_send, y_recv, dy_send, dy_recv, dz_send, dz_recv, dx_send, dx_recv, dc_send, dc_recv,
    pz_send, pz_recv, px_send, px_recv, pc_send, pc_recv, x_word, beside_in, all_in,
):
    m = lax.axis_index("gz")
    r = lax.axis_index("row")
    c = lax.axis_index("col")
    width = a_ref.shape[0]
    span = fin.shape[3]
    blocks = width // 128

    def layer(k):
        return lax.rem(m + k + LAYERS, LAYERS)

    def row_peer(k):
        return lax.rem(r + k + grid_rows, grid_rows)

    def col_peer(k):
        return lax.rem(c + k + grid_cols, grid_cols)

    other_core = c + 1 - 2 * lax.rem(c, 2)

    def in_line(here, step, count):
        return jnp.logical_and(here + step >= 0, here + step < count)

    barrier = pltpu.get_barrier_semaphore()
    for k in range(1, LAYERS):
        pl.semaphore_signal(barrier, inc=1, device_id=(layer(k), r, c), device_id_type=MESH)
    sides = [(r, 1, grid_rows), (r, -1, grid_rows), (c, 2, grid_cols), (c, -2, grid_cols)]

    def side(i):
        step = sides[i][1]
        place = (m, row_peer(step), c) if i < 2 else (m, r, col_peer(step))
        return place, in_line(*sides[i])

    for i in range(4):
        place, there = side(i)

        @pl.when(jnp.logical_and(there, m == 0))
        def _(place=place):
            pl.semaphore_signal(barrier, inc=1, device_id=place, device_id_type=MESH)

    pl.semaphore_signal(barrier, inc=1, device_id=(m, r, other_core), device_id_type=MESH)

    small = [
        pltpu.make_async_copy(x, y, load_sem.at[16 + i])
        for i, (x, y) in enumerate(((diag_hbm, diag_ref), (pattern_hbm, pattern_ref), (pivot_hbm, pivot_ref)))
    ]

    def load_panel(k, h):
        block = k * 2 + h
        return pltpu.make_async_copy(
            (column_ref, row_ref)[h].at[pl.ds(pl.multiple_of(k * PANEL, PANEL), PANEL), :],
            w.at[k, h, pl.ds(0, PANEL), :],
            load_sem.at[8 + block],
        )

    def load_front(k, h):
        block = k * 2 + h
        return pltpu.make_async_copy(
            schur_ref.at[pl.ds(pl.multiple_of(block * BS, BS), BS), :],
            w.at[k, h, pl.ds(PANEL, BS), :],
            load_sem.at[block],
        )

    order = [(layer(k), h) for k in (2, 1, -1, 0) for h in range(2)]
    small[0].start()
    for k, h in order:
        load_panel(k, h).start()
    for load in small[1:]:
        load.start()
    for k, h in order:
        load_front(k, h).start()

    def ring(t, d, s):
        step = 1 - 2 * d
        to = layer(step)
        first, count = SUBS[s]
        rows = pl.ds(first, count)
        if t == 1:
            src, dst = w.at[layer(2), d, rows], rs1.at[d, rows]
        elif t == 2:
            src, dst = w.at[to, 1 - d, rows], rsx.at[d, 1 - d, rows]
        elif t == 3:
            src, dst = w.at[to, d, rows], rsx.at[d, d, rows]
        elif t == 4:
            src = dst = fin.at[m, d, rows]
        elif t == 5:
            src = dst = fin.at[m, 1 - d, rows]
        else:
            src = dst = fin.at[layer(-step), d, rows]
        return pltpu.make_async_remote_copy(
            src_ref=src, dst_ref=dst, send_sem=y_send.at[t - 1, d, s], recv_sem=y_recv.at[t - 1, d, s],
            device_id=(to, r, c), device_id_type=MESH,
        )

    def add_opposite(s):
        first, count = SUBS[s]
        rows = pl.ds(first, count)
        for d in range(2):
            ring(1, d, s).wait_recv()
            to = layer(1 - 2 * d)
            w[to, d, rows, :] = w[to, d, rows, :] + rs1[d, rows, :]
            ring(3, d, s).start()

    def finish_sum(s):
        first, count = SUBS[s]
        rows = pl.ds(first, count)
        for d in range(2):
            ring(2, d, s).wait_recv()
            ring(3, d, s).wait_recv()
        for h in range(2):
            fin[m, h, rows, :] = w[m, h, rows, :] + rsx[0, h, rows, :] + rsx[1, h, rows, :]
        for t in (4, 5):
            for d in range(2):
                ring(t, d, s).start()

    def pass_on(s):
        for d in range(2):
            ring(4, d, s).wait_recv()
            ring(6, d, s).start()

    def arrived(s):
        for d in range(2):
            ring(5, d, s).wait_recv()
            ring(6, d, s).wait_recv()

    def diag_y(k):
        return pltpu.make_async_remote_copy(
            src_ref=layer_diag.at[m], dst_ref=layer_diag.at[m], send_sem=dy_send.at[k - 1], recv_sem=dy_recv.at[k - 1],
            device_id=(layer(k), r, c), device_id_type=MESH,
        )

    stages = [[k for k in stage if k < grid_rows] for stage in ((1,), (2,), (3, 4), (5, 6, 7))]

    def along_z(k, act):
        for d in range(2):
            to = r + k * (1 - 2 * d)
            copy = pltpu.make_async_remote_copy(
                src_ref=grid_diag.at[c, r], dst_ref=grid_diag.at[c, r],
                send_sem=dz_send.at[k - 1, d], recv_sem=dz_recv.at[k - 1, d],
                device_id=(m, lax.rem(to + grid_rows, grid_rows), c), device_id_type=MESH,
            )
            ahead, behind = to < grid_rows, to >= 0
            if act == "recv":
                ahead, behind = r - k * (1 - 2 * d) < grid_rows, r - k * (1 - 2 * d) >= 0

            @pl.when(jnp.logical_and(ahead, behind))
            def _(copy=copy):
                if act == "start":
                    copy.start()
                elif act == "recv":
                    copy.wait_recv()
                else:
                    copy.wait_send()

    def stage_z(i, act):
        for k in stages[i]:
            along_z(k, act)

    class AlongX:
        def __init__(self, ref, sems):
            self.ref, self.sems, self.steps = ref, sems, grid_cols // 4

        def part(self, j, d):
            block = col_peer(2 * j * (2 * d - 1))
            if j == self.steps - 1:
                half = self.ref.shape[1] // 2
                return self.ref.at[block, pl.ds(half * d, half)]
            return self.ref.at[block]

        def chip(self, j, d):
            ref = self.part(j, d)
            return pltpu.make_async_remote_copy(
                src_ref=ref, dst_ref=ref, send_sem=self.sems[0].at[j, d], recv_sem=self.sems[1].at[j, d],
                device_id=(m, r, col_peer(2 - 4 * d)), device_id_type=MESH,
            )

        def core(self, i):
            if i == 0:
                ref = self.ref.at[c]
            else:
                j, d = divmod(i - 1, 2)
                block = col_peer(2 * (j + 1) * (2 * d - 1))
                ref = self.ref.at[block]
                if j == self.steps - 1:
                    half = self.ref.shape[1] // 2
                    ref = self.ref.at[block, pl.ds(half * d, half)]
            return pltpu.make_async_remote_copy(
                src_ref=ref, dst_ref=ref, send_sem=self.sems[2].at[i], recv_sem=self.sems[3].at[i],
                device_id=(m, r, other_core), device_id_type=MESH,
            )

        def start(self):
            for d in range(2):
                if self.steps:
                    self.chip(0, d).start()
            self.core(0).start()

        def go_on(self, j):
            for d in range(2):
                self.chip(j, d).wait_recv()
                if j + 1 < self.steps:
                    self.chip(j + 1, d).start()
                self.core(1 + 2 * j + d).start()

        def finish(self):
            for i in range(1 + 2 * self.steps):
                self.core(i).wait_recv()

        def drain(self):
            for i in range(1 + 2 * self.steps):
                self.core(i).wait_send()
            for j in range(self.steps):
                for d in range(2):
                    self.chip(j, d).wait_send()

    diag_x = AlongX(grid_diag, (dx_send, dx_recv, dc_send, dc_recv))
    panel_x = AlongX(all_columns, (px_send, px_recv, pc_send, pc_recv))

    def send(t, s):
        for d in range(2):
            ring(t, d, s).start()

    def mask_front(k, h):
        load_front(k, h).wait()
        w[k, h, PANEL:HALF, :] = w[k, h, PANEL:HALF, :] * weights[pl.ds(k * 2 + h, 1), :]

    words = max(grid_cols // 2 - 2, 0)

    def word(i, act):
        for d in range(2):
            step = 2 - 4 * d
            @pl.when(in_line(c, step if act == "send" else -step, grid_cols))
            def _(d=d, step=step):
                if act == "send":
                    pl.semaphore_signal(
                        x_word.at[i, d], inc=1, device_id=(m, r, col_peer(step)), device_id_type=MESH
                    )
                else:
                    pl.semaphore_wait(x_word.at[i, d], 1)

    small[0].wait()
    layer_diag[m] = jnp.concatenate([diag_ref[:32, :], diag_ref[32:, :]], axis=1)
    beside = sum(in_line(*at).astype(jnp.int32) for at in sides)
    pl.semaphore_wait(barrier, LAYERS - 1 + 1 + jnp.where(m == 0, beside, 0))

    def layers_in():
        for i in range(4):
            place, there = side(i)

            @pl.when(jnp.logical_and(there, m == 0))
            def _(i=i, place=place):
                pl.semaphore_signal(beside_in.at[i ^ 1], inc=1, device_id=place, device_id_type=MESH)

    def sides_in():
        for i in range(4):
            _, there = side(i)

            @pl.when(jnp.logical_and(there, m == 0))
            def _(i=i):
                pl.semaphore_wait(beside_in.at[i], 1)

        @pl.when(m == 0)
        def _():
            for k in range(1, LAYERS):
                pl.semaphore_signal(all_in, inc=1, device_id=(layer(k), r, c), device_id_type=MESH)

        @pl.when(m != 0)
        def _():
            pl.semaphore_wait(all_in, 1)

    layers_in()
    for k in range(1, LAYERS):
        diag_y(k).start()
    for k, h in order[:6]:
        load_panel(k, h).wait()
    send(1, 0)
    send(2, 0)
    for load in small[1:]:
        load.wait()
    pattern = pattern_ref[...].astype(F32)
    weights[...] = jnp.concatenate(
        [jnp.broadcast_to(pattern[:, j : j + 1], (pattern.shape[0], BS)) for j in range(pattern.shape[1])], axis=1
    )
    for k, h in order[:2]:
        mask_front(k, h)
    send(1, 1)
    for k in range(1, LAYERS):
        diag_y(k).wait_recv()
    grid_diag[c, r] = layer_diag[0] + layer_diag[1] + layer_diag[2] + layer_diag[3]
    sides_in()
    stage_z(0, "start")
    if words:
        word(0, "send")
    add_opposite(0)
    send(1, 2)
    for i in range(words):
        word(i, "wait")
        if i + 1 < words:
            word(i + 1, "send")
    for k, h in order[2:6]:
        mask_front(k, h)
    stage_z(0, "recv")
    stage_z(1, "start")
    for k, h in order[6:]:
        load_panel(k, h).wait()
    finish_sum(0)
    send(1, 3)
    stage_z(1, "recv")
    stage_z(2, "start")
    pass_on(0)
    send(1, 4)
    for s in range(1, len(SUBS)):
        send(2, s)
    for k, h in order[6:]:
        mask_front(k, h)
    stage_z(2, "recv")
    stage_z(3, "start")
    stage_z(3, "recv")
    diag_x.start()

    far = grid_rows // 2

    def panel_z(j, d):
        step = 1 - 2 * d
        block = row_peer(-step * j)
        ref = all_rows.at[block, pl.ds(32 * d, 32)] if j == far - 1 else all_rows.at[block]
        return pltpu.make_async_remote_copy(
            src_ref=ref, dst_ref=ref, send_sem=pz_send.at[j, d], recv_sem=pz_recv.at[j, d],
            device_id=(m, row_peer(step), c), device_id_type=MESH,
        )

    def spread_panels(s):
        arrived(s)
        for k in range(LAYERS):
            all_columns[c, k * PANEL : (k + 1) * PANEL, :] = fin[k, 0, 0:PANEL, :]
            all_rows[r, k * PANEL : (k + 1) * PANEL, :] = fin[k, 1, 0:PANEL, :]
        for d in range(2):
            panel_z(0, d).start()
        panel_x.start()

    def rows_on(j):
        for d in range(2):
            panel_z(j - 1, d).wait_recv()
            panel_z(j, d).start()

    def columns_on(j):
        panel_x.go_on(j)

    add_opposite(1)
    add_opposite(2)
    for j in range(diag_x.steps):
        diag_x.go_on(j)
    spread_panels(0)
    add_opposite(3)
    add_opposite(4)
    diag_x.finish()

    low = lax.broadcasted_iota(jnp.int32, (grid_rows, 32, 128), 2) < 64
    for pair in range(grid_cols // 2):
        left, right = grid_diag[2 * pair], grid_diag[2 * pair + 1]
        lanes = slice(pair * 128, (pair + 1) * 128)
        full_diag[:, 0, :, lanes] = jnp.where(low, left, pltpu.roll(right, 64, 2))
        full_diag[:, 1, :, lanes] = jnp.where(low, pltpu.roll(left, 64, 2), right)
    chosen = (lax.broadcasted_iota(jnp.int32, (width, width), 0) == pivot_ref[...]).astype(BF16)
    full = full_diag[...].reshape(width, width)
    parts = [contract(chosen, x, 0, 0) for x in split3(full)]
    a_ref[...] = parts[0] + parts[1] + parts[2]

    slots = {
        (0, 0): [(finish_sum, 1)],
        (0, 1): [(rows_on, 1), (columns_on, 0)],
        (0, 3): [(finish_sum, 2)],
        (1, 1): [(finish_sum, 3), (columns_on, 1)],
        (1, 3): [(rows_on, 2)],
        (2, 0): [(finish_sum, 4)],
        (2, 3): [(rows_on, 3)],
        (3, 2): [(pass_on, 1)],
    }
    slots = {at: [
            (f, s) for f, s in work if not (f is rows_on and s >= far) and not (f is columns_on and s >= panel_x.steps)
        ]
        for at, work in slots.items()}

    def hook(i, at):
        for (block, place), work in slots.items():
            if place == at and block < blocks and work:
                @pl.when(i == block)
                def _(work=work):
                    for f, s in work:
                        f(s)

    def hooks_after(least, most):
        for (block, place), work in sorted(slots.items()):
            if least <= block <= most:
                for f, s in work:
                    f(s)

    @pl.loop(0, blocks)
    def _(i):
        eliminate_block(a_ref, d_ref, up_ref, i, hook)

    hooks_after(blocks, 4)

    strip = a_ref[pl.ds(pl.multiple_of(c * 64, 64), 64), pl.ds(pl.multiple_of((r // 2) * 128, 128), 128)]
    diagonal = up_ref[c // 2, pl.ds(pl.multiple_of(lax.rem(c, 2) * 64, 64), 64), :]
    strip = jnp.where(r // 2 > c // 2, strip, jnp.where(r // 2 == c // 2, diagonal, 0.0))
    odd = lax.rem(r, 2) == 1
    factor_out[...] = jnp.transpose(jnp.where(odd, pltpu.roll(strip, 64, 1), strip))[:64, :]

    inverse = jnp.where(
        lax.broadcasted_iota(jnp.int32, (width, width), 1) // 128
        <= lax.broadcasted_iota(jnp.int32, (width, width), 0) // 128,
        a_ref[...],
        0.0,
    )
    inv = split2(inverse)
    panel_x.finish()
    tile = 256

    def panel_tile(target, source, factor):
        @pl.loop(0, span // tile)
        def _(t):
            lanes = pl.ds(pl.multiple_of(t * tile, tile), tile)
            target[:, lanes] = dot3(factor, split2(source[:, :, lanes].reshape(width, tile)))

    panel_tile(left_x, all_columns, inv)
    lower_out[...] = left_x[pl.ds(pl.multiple_of(c * 64, 64), 64), :]
    pass_on(2)
    parts = [contract(x, chosen, 1, 1) for x in split3(inverse)]
    inv_pivot = split2(parts[0] + parts[1] + parts[2])
    for d in range(2):
        panel_z(far - 1, d).wait_recv()
    panel_tile(right_x, all_rows, inv_pivot)
    upper_out[...] = right_x[pl.ds(pl.multiple_of(r * 64, 64), 64), :]

    pass_on(3)

    right = split2(right_x[...])

    @pl.loop(0, span // BS)
    def _(t):
        rows = pl.ds(pl.multiple_of(t * BS, BS), BS)
        update[t, :, :] = dot3(split2(jnp.transpose(left_x[:, rows])), right)

    def subtract(k, h, s):
        first, count = SUBS[s]
        into = pl.ds(first - PANEL, count)
        update[k * 2 + h, into, :] = fin[k, h, pl.ds(first, count), :] - update[k * 2 + h, into, :]

    pass_on(4)
    for s in range(1, len(SUBS)):
        for h in range(2):
            subtract(m, h, s)
    for s in range(1, len(SUBS)):
        for d in range(2):
            ring(5, d, s).wait_recv()
        for k in (1, -1):
            for h in range(2):
                subtract(layer(k), h, s)
    for s in range(1, len(SUBS)):
        for d in range(2):
            ring(6, d, s).wait_recv()
        for h in range(2):
            subtract(layer(2), h, s)

    for s in range(len(SUBS)):
        for t in range(1, 7):
            for d in range(2):
                ring(t, d, s).wait_send()
    for k in range(1, LAYERS):
        diag_y(k).wait_send()
    for i in range(len(stages)):
        stage_z(i, "send")
    diag_x.drain()
    panel_x.drain()
    for j in range(far):
        for d in range(2):
            panel_z(j, d).wait_send()


def store_kernel(*refs):
    ins, outs, sem = refs[:4], refs[4:8], refs[8]
    copies = [pltpu.make_async_copy(ins[3].at[i], outs[3].at[i], sem.at[3 + i]) for i in range(ins[3].shape[0])]
    copies += [pltpu.make_async_copy(ins[i], outs[i], sem.at[i]) for i in range(3)]
    for copy in copies:
        copy.start()
    for copy in copies:
        copy.wait()


def per_device(diag_parts, column_parts, row_parts, schur_parts, block_pattern, pivot_order):
    rows_dev, cols_dev = schur_parts.shape[1:]
    width = pivot_order.shape[0]
    grid_rows, grid_cols = lax.axis_size("row"), lax.axis_size("col")
    vmem = pl.BlockSpec(memory_space=pltpu.VMEM)
    anywhere = pl.BlockSpec(memory_space=pl.ANY)
    dma = pltpu.SemaphoreType.DMA
    subs = len(SUBS)
    chips = max(grid_cols // 4, 1)
    shapes = (
        diag_parts.shape[1:],
        column_parts.shape[:0:-1],
        row_parts.shape[1:],
        (rows_dev // BS, BS, cols_dev),
    )
    held = pl.pallas_call(
        functools.partial(kernel, grid_rows, grid_cols),
        out_shape=tuple(pltpu.VMEM(shape, F32) for shape in shapes),
        in_specs=[pl.BlockSpec(memory_space=pltpu.HBM)] * 6,
        out_specs=[vmem] * 4,
        scratch_shapes=[
            pltpu.VMEM(diag_parts.shape[1:], F32),
            pltpu.VMEM(block_pattern.shape[1:], jnp.int32),
            pltpu.VMEM((1, width), jnp.int32),
            pltpu.VMEM((LAYERS, 2, HALF, cols_dev), F32),
            pltpu.VMEM((LAYERS, 2, HALF, cols_dev), F32),
            pltpu.VMEM((2, HALF, cols_dev), F32),
            pltpu.VMEM((2, 2, HALF, cols_dev), F32),
            pltpu.VMEM((rows_dev // BS, cols_dev), F32),
            pltpu.VMEM((LAYERS, 32, 128), F32),
            pltpu.VMEM((grid_cols, grid_rows, 32, 128), F32),
            pltpu.VMEM((grid_rows, 2, 32, width), F32),
            pltpu.VMEM((grid_cols, 64, rows_dev), F32),
            pltpu.VMEM((grid_rows, 64, cols_dev), F32),
            pltpu.VMEM((width, width), F32),
            pltpu.VMEM((128, 128), F32),
            pltpu.VMEM((width // 128, 128, 128), F32),
            pltpu.VMEM((width, rows_dev), F32),
            pltpu.VMEM((width, cols_dev), F32),
            dma((19,)),
            dma((6, 2, subs)),
            dma((6, 2, subs)),
            dma((LAYERS - 1,)),
            dma((LAYERS - 1,)),
            dma((grid_rows - 1, 2)),
            dma((grid_rows - 1, 2)),
            dma((chips, 2)),
            dma((chips, 2)),
            dma((1 + 2 * chips,)),
            dma((1 + 2 * chips,)),
            dma((grid_rows // 2, 2)),
            dma((grid_rows // 2, 2)),
            dma((chips, 2)),
            dma((chips, 2)),
            dma((1 + 2 * chips,)),
            dma((1 + 2 * chips,)),
            pltpu.SemaphoreType.REGULAR((2, 2)),
            pltpu.SemaphoreType.REGULAR((4,)),
            pltpu.SemaphoreType.REGULAR,
        ],
        compiler_params=pltpu.CompilerParams(
            collective_id=0, has_side_effects=True, vmem_limit_bytes=48 << 20
        ),
    )(
        *(
            pltpu.with_memory_space_constraint(x, pltpu.HBM)
            for x in (
                diag_parts[0],
                block_pattern[0],
                pivot_order.reshape(1, width),
                column_parts[0].T,
                row_parts[0],
                schur_parts[0],
            )
        )
    )
    factor, lower_t, upper, schur = pl.pallas_call(
        store_kernel,
        out_shape=tuple(jax.ShapeDtypeStruct(shape, F32) for shape in shapes),
        in_specs=[vmem] * 4,
        out_specs=[anywhere] * 4,
        scratch_shapes=[dma((3 + rows_dev // BS,))],
        compiler_params=pltpu.CompilerParams(vmem_limit_bytes=8 << 20),
    )(*held)
    return factor, lower_t.T, upper, schur.reshape(rows_dev, cols_dev)


def solution(mesh):
    placed = (
        P("gz", "row", "col"),
        P("gz", "row", "col"),
        P("gz", "row", "col"),
        P("gz", "row", "col"),
        P("gz", "row", "col"),
        P(),
    )
    return jax.shard_map(
        per_device,
        mesh=mesh,
        in_specs=placed,
        out_specs=(P("row", "col"), P("row", "col"), P("row", "col"), P("row", "col")),
        check_vma=False,
    )
```

profile of v0, /device:TPU:2, one launch (start us, length us, event | category | flops | bytes accessed | tf_op | source)
XLA Modules:
  0.0 87.3 jit_solution(1215014474484627222)
XLA Ops:
  0.6 84.4 %shard_map.93 = (f32[64,64]{1,0:T(8,128)S(1)}, f32[64,1024]{1,0:T(8,128)S(1)}, f32[64,1024]{1,0:T(8,128)S(1)}, f32[8,128,1024]{2,1,0:T(8,128)S(1)}) custom-call(f32[64,64]{1,0:T(8,128)} %bitcast.13, s32[8,8]{1,0:T(8,128)} %bitcast.14, s32[1,512]{1,0:T(1,128)} %bitcast.15, f32[64,1024]{1,0:T(8,128)} %bitcast.11, f32[64,1024]{1,0:T(8,128)} %bitcast.12, ...), custom_call_target="tpu_custom_call" | custom-call | tf_op jit(solution)/shard_map/pallas_call | solution.py:624
  85.0 2.3 %shard_map.94 = (f32[64,64]{1,0:T(8,128)}, f32[64,1024]{1,0:T(8,128)}, f32[64,1024]{1,0:T(8,128)}, f32[8,128,1024]{2,1,0:T(8,128)}) custom-call(f32[64,64]{1,0:T(8,128)S(1)} %get-tuple-element.12.refs_0_, f32[64,1024]{1,0:T(8,128)S(1)} %get-tuple-element.13.refs_1_, f32[64,1024]{1,0:T(8,128)S(1)} %get-tuple-element.14.refs_2_, ...), custom_call_target="tpu_custom_call" | custom-call | tf_op jit(solution)/shard_map/pallas_call | solution.py:685
where the time goes:
time: 87.4 us; the launch traced here: 87.3 us
  Pallas kernels  86.6 us (99%)
    pallas_call x1, Pallas kernels, per_device(): pl.pallas_call(functools.partial(kernel, grid_rows, grid_cols), out_shape...  84.4 us
    pallas_call x1, Pallas kernels, per_device(): pl.pallas_call(store_kernel, out_shape=tuple((jax.ShapeDtypeStruct(shape,...  2.27 us

commit v1 on v0

--- a/solution.py
+++ b/solution.py
@@ -11,7 +11,7 @@
 LAYERS = 4
 PANEL = 16
 HALF = PANEL + BS
-SUBS = ((0, 16), (16, 32), (48, 32), (80, 32), (112, 32))
+SUBS = ((0, 16), (16, 64), (80, 64))
 HI = lax.Precision.HIGHEST
 F32 = jnp.float32
 BF16 = jnp.bfloat16
@@ -421,18 +421,15 @@
     stage_z(1, "start")
     for k, h in order[6:]:
         load_panel(k, h).wait()
-    finish_sum(0)
-    send(1, 3)
+        mask_front(k, h)
     stage_z(1, "recv")
     stage_z(2, "start")
-    pass_on(0)
-    send(1, 4)
-    for s in range(1, len(SUBS)):
-        send(2, s)
-    for k, h in order[6:]:
-        mask_front(k, h)
+    finish_sum(0)
+    send(2, 1)
     stage_z(2, "recv")
     stage_z(3, "start")
+    pass_on(0)
+    send(2, 2)
     stage_z(3, "recv")
     diag_x.start()
 
@@ -465,12 +462,10 @@
         panel_x.go_on(j)
 
     add_opposite(1)
-    add_opposite(2)
     for j in range(diag_x.steps):
         diag_x.go_on(j)
     spread_panels(0)
-    add_opposite(3)
-    add_opposite(4)
+    add_opposite(2)
     diag_x.finish()
 
     low = lax.broadcasted_iota(jnp.int32, (grid_rows, 32, 128), 2) < 64
@@ -487,10 +482,9 @@
     slots = {
         (0, 0): [(finish_sum, 1)],
         (0, 1): [(rows_on, 1), (columns_on, 0)],
-        (0, 3): [(finish_sum, 2)],
-        (1, 1): [(finish_sum, 3), (columns_on, 1)],
+        (1, 1): [(columns_on, 1)],
+        (1, 2): [(finish_sum, 2)],
         (1, 3): [(rows_on, 2)],
-        (2, 0): [(finish_sum, 4)],
         (2, 3): [(rows_on, 3)],
         (3, 2): [(pass_on, 1)],
     }
@@ -543,7 +537,6 @@
 
     panel_tile(left_x, all_columns, inv)
     lower_out[...] = left_x[pl.ds(pl.multiple_of(c * 64, 64), 64), :]
-    pass_on(2)
     parts = [contract(x, chosen, 1, 1) for x in split3(inverse)]
     inv_pivot = split2(parts[0] + parts[1] + parts[2])
     for d in range(2):
@@ -551,7 +544,7 @@
     panel_tile(right_x, all_rows, inv_pivot)
     upper_out[...] = right_x[pl.ds(pl.multiple_of(r * 64, 64), 64), :]
 
-    pass_on(3)
+    pass_on(2)
 
     right = split2(right_x[...])
 
@@ -560,31 +553,14 @@
         rows = pl.ds(pl.multiple_of(t * BS, BS), BS)
         update[t, :, :] = dot3(split2(jnp.transpose(left_x[:, rows])), right)
 
-    def subtract(k, h, s):
-        first, count = SUBS[s]
-        into = pl.ds(first - PANEL, count)
-        update[k * 2 + h, into, :] = fin[k, h, pl.ds(first, count), :] - update[k * 2 + h, into, :]
-
-    pass_on(4)
-    for s in range(1, len(SUBS)):
-        for h in range(2):
-            subtract(m, h, s)
-    for s in range(1, len(SUBS)):
-        for d in range(2):
-            ring(5, d, s).wait_recv()
-        for k in (1, -1):
-            for h in range(2):
-                subtract(layer(k), h, s)
-    for s in range(1, len(SUBS)):
-        for d in range(2):
-            ring(6, d, s).wait_recv()
-        for h in range(2):
-            subtract(layer(2), h, s)
-
-    for s in range(len(SUBS)):
-        for t in range(1, 7):
-            for d in range(2):
-                ring(t, d, s).wait_send()
+    def sent(steps, pieces):
+        for s in pieces:
+            for t in steps:
+                for d in range(2):
+                    ring(t, d, s).wait_send()
+
+    sent((1, 2, 3), range(len(SUBS)))
+    sent((4, 5, 6), range(1))
     for k in range(1, LAYERS):
         diag_y(k).wait_send()
     for i in range(len(stages)):
@@ -594,6 +570,28 @@
     for j in range(far):
         for d in range(2):
             panel_z(j, d).wait_send()
+
+    def subtract(k, h, s):
+        first, count = SUBS[s]
+        into = pl.ds(first - PANEL, count)
+        update[k * 2 + h, into, :] = fin[k, h, pl.ds(first, count), :] - update[k * 2 + h, into, :]
+
+    for s in range(1, len(SUBS)):
+        for h in range(2):
+            subtract(m, h, s)
+    for s in range(1, len(SUBS)):
+        for d in range(2):
+            ring(5, d, s).wait_recv()
+        for k in (1, -1):
+            for h in range(2):
+                subtract(layer(k), h, s)
+    sent((4, 5), range(1, len(SUBS)))
+    for s in range(1, len(SUBS)):
+        for d in range(2):
+            ring(6, d, s).wait_recv()
+        for h in range(2):
+            subtract(layer(2), h, s)
+    sent((6,), range(1, len(SUBS)))
 
 
 def store_kernel(*refs):

time: 87.4 us -> 86.1 us (0.985)
  Pallas kernels: 86.6 us -> 85.4 us
    pallas_call x1, Pallas kernels: 84.4 us -> 83.1 us  [per_device(): pl.pallas_call(functools.partial(kernel, grid_rows, grid_cols), out_shape...]
where the time goes in v1:
time: 86.1 us; the launch traced here: 86 us
  Pallas kernels  85.4 us (99%)
    pallas_call x1, Pallas kernels, per_device(): pl.pallas_call(functools.partial(kernel, grid_rows, grid_cols), out_shape...  83.1 us
    pallas_call x1, Pallas kernels, per_device(): pl.pallas_call(store_kernel, out_shape=tuple((jax.ShapeDtypeStruct(shape,...  2.27 us

profile of v1, /device:TPU:2, one launch (start us, length us, event | category | flops | bytes accessed | tf_op | source)
XLA Modules:
  0.0 86.0 jit_solution(1593433166589614515)
XLA Ops:
  0.6 83.1 %shard_map.93 = (f32[64,64]{1,0:T(8,128)S(1)}, f32[64,1024]{1,0:T(8,128)S(1)}, f32[64,1024]{1,0:T(8,128)S(1)}, f32[8,128,1024]{2,1,0:T(8,128)S(1)}) custom-call(f32[64,64]{1,0:T(8,128)} %bitcast.13, s32[8,8]{1,0:T(8,128)} %bitcast.14, s32[1,512]{1,0:T(1,128)} %bitcast.15, f32[64,1024]{1,0:T(8,128)} %bitcast.11, f32[64,1024]{1,0:T(8,128)} %bitcast.12, ...), custom_call_target="tpu_custom_call" | custom-call | tf_op jit(solution)/shard_map/pallas_call | solution.py:622
  83.7 2.3 %shard_map.94 = (f32[64,64]{1,0:T(8,128)}, f32[64,1024]{1,0:T(8,128)}, f32[64,1024]{1,0:T(8,128)}, f32[8,128,1024]{2,1,0:T(8,128)}) custom-call(f32[64,64]{1,0:T(8,128)S(1)} %get-tuple-element.12.refs_0_, f32[64,1024]{1,0:T(8,128)S(1)} %get-tuple-element.13.refs_1_, f32[64,1024]{1,0:T(8,128)S(1)} %get-tuple-element.14.refs_2_, ...), custom_call_target="tpu_custom_call" | custom-call | tf_op jit(solution)/shard_map/pallas_call | solution.py:683

commit v2 on v1

--- a/solution.py
+++ b/solution.py
@@ -140,7 +140,7 @@
         return jnp.logical_and(here + step >= 0, here + step < count)
 
     barrier = pltpu.get_barrier_semaphore()
-    for k in range(1, LAYERS):
+    for k in (1, 3, 2):
         pl.semaphore_signal(barrier, inc=1, device_id=(layer(k), r, c), device_id_type=MESH)
     sides = [(r, 1, grid_rows), (r, -1, grid_rows), (c, 2, grid_cols), (c, -2, grid_cols)]
 
@@ -596,8 +596,7 @@
 
 def store_kernel(*refs):
     ins, outs, sem = refs[:4], refs[4:8], refs[8]
-    copies = [pltpu.make_async_copy(ins[3].at[i], outs[3].at[i], sem.at[3 + i]) for i in range(ins[3].shape[0])]
-    copies += [pltpu.make_async_copy(ins[i], outs[i], sem.at[i]) for i in range(3)]
+    copies = [pltpu.make_async_copy(ins[i], outs[i], sem.at[i]) for i in (3, 0, 1, 2)]
     for copy in copies:
         copy.start()
     for copy in copies:
@@ -685,7 +684,7 @@
         out_shape=tuple(jax.ShapeDtypeStruct(shape, F32) for shape in shapes),
         in_specs=[vmem] * 4,
         out_specs=[anywhere] * 4,
-        scratch_shapes=[dma((3 + rows_dev // BS,))],
+        scratch_shapes=[dma((4,))],
         compiler_params=pltpu.CompilerParams(vmem_limit_bytes=8 << 20),
     )(*held)
     return factor, lower_t.T, upper, schur.reshape(rows_dev, cols_dev)

time: 86.1 us -> 86 us (level)
  no operation moved by 1% of the time
where the time goes in v2:
time: 86 us
  Pallas kernels  85.3 us (99%)
    pallas_call x1, Pallas kernels, per_device(): pl.pallas_call(functools.partial(kernel, grid_rows, grid_cols), out_shape...  83.1 us
    pallas_call x1, Pallas kernels, per_device(): pl.pallas_call(store_kernel, out_shape=tuple((jax.ShapeDtypeStruct(shape,...  2.21 us

profile of v2, /device:TPU:2, one launch (start us, length us, event | category | flops | bytes accessed | tf_op | source)
XLA Modules:
  0.0 86.0 jit_solution(8097761362369183866)
XLA Ops:
  0.6 83.1 %shard_map.93 = (f32[64,64]{1,0:T(8,128)S(1)}, f32[64,1024]{1,0:T(8,128)S(1)}, f32[64,1024]{1,0:T(8,128)S(1)}, f32[8,128,1024]{2,1,0:T(8,128)S(1)}) custom-call(f32[64,64]{1,0:T(8,128)} %bitcast.13, s32[8,8]{1,0:T(8,128)} %bitcast.14, s32[1,512]{1,0:T(1,128)} %bitcast.15, f32[64,1024]{1,0:T(8,128)} %bitcast.11, f32[64,1024]{1,0:T(8,128)} %bitcast.12, ...), custom_call_target="tpu_custom_call" | custom-call | tf_op jit(solution)/shard_map/pallas_call | solution.py:621
  83.8 2.2 %shard_map.94 = (f32[64,64]{1,0:T(8,128)}, f32[64,1024]{1,0:T(8,128)}, f32[64,1024]{1,0:T(8,128)}, f32[8,128,1024]{2,1,0:T(8,128)}) custom-call(f32[64,64]{1,0:T(8,128)S(1)} %get-tuple-element.12.refs_0_, f32[64,1024]{1,0:T(8,128)S(1)} %get-tuple-element.13.refs_1_, f32[64,1024]{1,0:T(8,128)S(1)} %get-tuple-element.14.refs_2_, ...), custom_call_target="tpu_custom_call" | custom-call | tf_op jit(solution)/shard_map/pallas_call | solution.py:682
